TPU v7x, 32 devices: a whole 2x2x4 slice. The times are simulated.
32 devices in a mesh: screen: 4 (over z), depth: 8 (over y, x, core).
Axes of the slice: x: 2, y: 2, z: 4, core: 2. Of those that a mesh axis runs over, the one named last changes fastest.
Arguments:
- density: bfloat16 [64, 64, 512], P('depth', None, 'screen'), as said below
- bin_index: int32 [64, 64, 512], P('depth', None, 'screen'), may hold values from 0 to 255
- transfer: bfloat16 [4, 256], replicated, may hold values from 0.049804688 to 1
- view_side: int32 [512], P('screen'), may hold values 0 or 1
Outputs:
- image: float32 [4, 64, 512], P(None, 'depth', 'screen')
Inputs may be any that keep to these rules, and one draw needn't show every extreme that they name: Up to bfloat16 rounding a voxel's density lies between bin_index / 256 and (bin_index + 1) / 256.
All inputs are finite; a program needn't handle non-finite values. No bound on the sum of `view_side` on one device may be relied on, other than what follows from the above.
Results may differ from a plain program's by a relative error of at most 0.0003.
Values may be sent and summed in bfloat16 or wider, within the bound.
A program may use at most 64 MiB of HBM per device.

v0:
```python
import jax
import jax.numpy as jnp
from jax import lax
from jax.sharding import PartitionSpec as P

LIGHT_DIRECTION = (0.36, 0.48, 0.8)
AMBIENT = 0.3
DIFFUSE = 0.7
OPTICAL = 4.0


def padded_2(x, sides, width):
    for axis, dim in sides:
        devices, length = (lax.axis_size(axis), x.shape[dim])
        up = [(i, (i + 1) % devices) for i in range(devices - 1)]
        down = [(j, i) for i, j in up]
        last = lax.slice_in_dim(x, length - width, length, axis=dim)
        initial = lax.slice_in_dim(x, 0, width, axis=dim)
        before = lax.ppermute(last, axis, up)
        after = lax.ppermute(initial, axis, down)
        x = jnp.concatenate([before, x, after], axis=dim)
    return x


def centred_diff(field, axis):
    length = field.shape[axis] - 4

    def shifted(offset):
        return lax.slice_in_dim(field, 2 + offset, 2 + offset + length, axis=axis)

    return (8.0 * (shifted(1) - shifted(-1)) - (shifted(2) - shifted(-2))) / 12.0


def shading_of(padded):
    field = padded.astype(jnp.float32)
    grad_depth = centred_diff(field[:, 2:-2, 2:-2], 0)
    grad_rows = centred_diff(field[2:-2, :, 2:-2], 1)
    grad_cols = centred_diff(field[2:-2, 2:-2, :], 2)
    light_dot = (
        LIGHT_DIRECTION[0] * grad_cols
        + LIGHT_DIRECTION[1] * grad_rows
        + LIGHT_DIRECTION[2] * grad_depth
    )
    squared = grad_cols * grad_cols + grad_rows * grad_rows + grad_depth * grad_depth
    return AMBIENT + DIFFUSE * jnp.abs(light_dot) / jnp.sqrt(squared + 1.0)


def lookup(bin_index, transfer):
    voxel_count = bin_index.size
    block_len = voxel_count
    while block_len > 32768 and block_len % 2 == 0:
        block_len = block_len // 2
    flattened = bin_index.reshape(voxel_count // block_len, block_len)
    levels = lax.broadcasted_iota(jnp.int32, (transfer.shape[1], 1), 0)

    def lookup_block(block_bins):
        onehot = (levels == block_bins[None, :]).astype(jnp.bfloat16)
        return jnp.dot(transfer, onehot, preferred_element_type=jnp.float32)

    looked = lax.map(lookup_block, flattened)
    return jnp.transpose(looked, (1, 0, 2)).reshape((4,) + bin_index.shape)


def on_device(density, bin_index, transfer, view_side):
    padded = padded_2(density, (("screen", 2), ("depth", 0)), 2)
    padded = jnp.pad(padded, ((0, 0), (2, 2), (0, 0)))
    shading = shading_of(padded)
    looked = lookup(bin_index, transfer)
    depth_total = density.shape[0] * lax.axis_size("depth")
    optical = looked[3] * (OPTICAL / depth_total)
    opacity = 1.0 - jnp.exp(-optical)
    running = jnp.cumsum(optical, axis=0)
    through = running[-1]
    before = jnp.where(view_side == 0, running - optical, through[None] - running)
    weight = jnp.exp(-before) * opacity * shading
    colour = jnp.sum(looked[:3] * weight[None], axis=1)
    partial_value = jnp.concatenate([colour, jnp.exp(-through)[None]], axis=0)
    count = lax.axis_size("depth")
    row_total = partial_value.shape[1]
    block_rows = row_total // count
    columns = partial_value.shape[2]
    tiles = partial_value.reshape(4, count, block_rows, columns)
    arrived = lax.all_to_all(tiles, "depth", split_axis=1, concat_axis=1, tiled=True)
    transmit = arrived[3]
    ones_row = jnp.ones_like(transmit[:1])
    inclusive = jnp.cumprod(transmit, axis=0)
    ahead_low = jnp.concatenate([ones_row, inclusive[:-1]], axis=0)
    reverse_incl = jnp.cumprod(transmit[::-1], axis=0)[::-1]
    ahead_high = jnp.concatenate([reverse_incl[1:], ones_row], axis=0)
    ahead = jnp.where(view_side == 0, ahead_low, ahead_high)
    final_colour = jnp.sum(arrived[:3] * ahead[None], axis=1)
    image = jnp.concatenate([final_colour, 1.0 - inclusive[-1:]], axis=0)
    return image


def solution(mesh):
    placed = (P("depth", None, "screen"), P("depth", None, "screen"), P(), P("screen"))
    return jax.shard_map(
        on_device, mesh=mesh, in_specs=placed, out_specs=P(None, "depth", "screen"), check_vma=False
    )
```

profile of v0, /device:TPU:0, one launch (start us, length us, event | category | flops | bytes accessed | tf_op | source)
XLA Modules:
  0.0 42.9 jit_solution(17944315282447882659)
XLA Ops:
  0.0 0.0 copy-start.3
  0.0 1.1 %fusion.19 = (bf16[8,64,2]{2,1,0:T(8,128)(2,1)S(1)}, bf16[8,64,2]{2,1,0:T(8,128)(2,1)S(1)}) fusion(bf16[8,64,128]{2,1,0:T(8,128)(2,1)} %param.6), kind=kLoop, calls=%fused_computation.46 | loop fusion | bytes 8192 | tf_op jit(solution)/shard_map/slice | solution.py:17
  1.1 1.3 %collective-permute-start.1 = (bf16[8,64,2]{2,1,0:T(8,128)(2,1)S(1)}, bf16[8,64,2]{2,1,0:T(8,128)(2,1)S(1)}, u32[]{:S(2)}, u32[]{:S(2)}) collective-permute-start(bf16[8,64,2]{2,1,0:T(8,128)(2,1)S(1)} %get-tuple-element.56), channel_id=1, source_target_pairs={{8,0},{16,8},{24,16},{9,1},{17,9},{25,17},{10,2},{18,10},{26,18},{... | collective-permute-start | bytes 6152 | tf_op jit(solution)/shard_map/ppermute | solution.py:20
  2.4 5.6 %collective-permute-start = (bf16[8,64,2]{2,1,0:T(8,128)(2,1)S(1)}, bf16[8,64,2]{2,1,0:T(8,128)(2,1)S(1)}, u32[]{:S(2)}, u32[]{:S(2)}) collective-permute-start(bf16[8,64,2]{2,1,0:T(8,128)(2,1)S(1)} %get-tuple-element.55), channel_id=1, source_target_pairs={{0,8},{8,16},{16,24},{1,9},{9,17},{17,25},{2,10},{10,18},{18,26},{... | collective-permute-start | bytes 6152 | tf_op jit(solution)/shard_map/ppermute | solution.py:19
  8.0 1.1 %reshape.14 = s32[2,32768]{1,0:T(2,128)S(1)} reshape(s32[8,64,128]{2,1,0:T(8,128)} %param.7) | data formatting | bytes 524288 | tf_op jit(solution)/shard_map/reshape | solution.py:53
  9.1 0.0 copy-done.3
  9.1 10.4 %while.11 = (s32[]{:T(128)}, f32[2,4,32768]{2,1,0:T(4,128)S(1)}, s32[2,32768]{1,0:T(2,128)S(1)}, bf16[4,256]{1,0:T(4,128)(2,1)S(1)}, s32[]{:T(128)}) while((s32[]{:T(128)}, f32[2,4,32768]{2,1,0:T(4,128)S(1)}, s32[2,32768]{1,0:T(2,128)S(1)}, bf16[4,256]{1,0:T(4,128)(2,1)S(1)}, s32[]{:T(128)}) %tuple.27), condition=%wide.region_1.2_spmd.clone, body=%wide.region_0.1_spmd.clone.sunk | while | flops 75497472 | bytes 919629 | solution.py:60
  9.1 0.1 constant_dynamic-slice_fusion.2
  9.2 5.1 %fusion.28 = f32[2,4,32768]{2,1,0:T(4,128)S(1)} fusion(f32[2,4,32768]{2,1,0:T(4,128)S(1)} %get-tuple-element.88, s32[]{:T(128)S(6)} %copy.12, bf16[4,256]{1,0:T(4,128)(2,1)S(1)} %get-tuple-element.95, s32[32768]{0:T(1024)S(1)} %bitcast.27), kind=kOutput, calls=%fused_computation.2.clone.1 | convolution fusion | flops 75497472 | bytes 657412 | tf_op jit(solution)/shard_map/while/body/eval_jaxpr/dot_general | solution.py:58
  14.3 0.1 constant_dynamic-slice_fusion.2
  14.4 5.1 %fusion.28 = f32[2,4,32768]{2,1,0:T(4,128)S(1)} fusion(f32[2,4,32768]{2,1,0:T(4,128)S(1)} %get-tuple-element.88, s32[]{:T(128)S(6)} %copy.12, bf16[4,256]{1,0:T(4,128)(2,1)S(1)} %get-tuple-element.95, s32[32768]{0:T(1024)S(1)} %bitcast.27), kind=kOutput, calls=%fused_computation.2.clone.1 | convolution fusion | flops 75497472 | bytes 657412 | tf_op jit(solution)/shard_map/while/body/eval_jaxpr/dot_general | solution.py:58
  19.5 0.0 copy-start
  19.5 0.0 copy-start.4
  19.5 0.3 slice_multiply_fusion
  19.9 0.3 fusion.20
  20.2 0.6 %slice_bitcast_fusion.1 = (f32[64,128]{1,0:T(8,128)}, f32[1,8,8,128]{3,2,1,0:T(8,128)}) fusion(f32[8,64,128]{2,1,0:T(8,128)S(1)} %fusion.20), kind=kLoop, calls=%fused_computation.41 | loop fusion | flops 8192 | bytes 98304 | tf_op jit(solution)/shard_map/sub | solution.py:74
  20.8 0.0 collective-permute-done.1
  20.8 0.0 collective-permute-done
  20.8 0.0 copy-done
  20.8 0.8 %pad_maximum_fusion.3 = (bf16[2,64,132]{2,1,0:T(8,128)(2,1)}, bf16[2,64,132]{2,1,0:T(8,128)(2,1)}) fusion(bf16[8,64,2]{2,1,0:T(8,128)(2,1)S(1)} %collective-permute-done.1, bf16[8,64,128]{2,1,0:T(8,128)(2,1)S(1)} %copy-done, bf16[8,64,2]{2,1,0:T(8,128)(2,1)S(1)} %collective-permute-done), kind=kLoop, calls=%fused_computation.37 | loop fusion | flops 202752 | bytes 202752 | tf_op jit(solution)/shard_map/slice | solution.py:17
  21.6 1.3 %collective-permute-start.3 = (bf16[2,64,132]{2,1,0:T(8,128)(2,1)}, bf16[2,64,132]{2,1,0:T(8,128)(2,1)}, u32[]{:S(2)}, u32[]{:S(2)}) collective-permute-start(bf16[2,64,132]{2,1,0:T(8,128)(2,1)} %get-tuple-element.52), channel_id=1, source_target_pairs={{1,0},{2,1},{3,2},{4,3},{5,4},{6,5},{7,6},{9,8},{10,9},{11,10},{12... | collective-permute-start | bytes 101384 | tf_op jit(solution)/shard_map/ppermute | solution.py:20
  22.9 3.7 %collective-permute-start.2 = (bf16[2,64,132]{2,1,0:T(8,128)(2,1)}, bf16[2,64,132]{2,1,0:T(8,128)(2,1)}, u32[]{:S(2)}, u32[]{:S(2)}) collective-permute-start(bf16[2,64,132]{2,1,0:T(8,128)(2,1)} %get-tuple-element.51), channel_id=1, source_target_pairs={{0,1},{1,2},{2,3},{3,4},{4,5},{5,6},{6,7},{8,9},{9,10},{10,11},{11... | collective-permute-start | bytes 101384 | tf_op jit(solution)/shard_map/ppermute | solution.py:19
  26.6 0.0 copy-done.4
  26.6 0.6 %copy.7 = f32[3,2,32768]{2,1,0:T(2,128)S(1)} copy(f32[3,2,32768]{2,0,1:T(4,128)S(1)} %bitcast.31) | data formatting | bytes 1572864 | tf_op jit(solution)/shard_map/slice | solution.py:76
  27.2 0.7 %slice.95 = f32[3,8,64,128]{3,2,1,0:T(8,128)S(1)} reshape(f32[3,2,32768]{2,1,0:T(2,128)S(1)} %copy.7) | data formatting | bytes 1572864 | tf_op jit(solution)/shard_map/slice | solution.py:76
  27.9 0.0 copy-start.1
  27.9 0.0 collective-permute-done.3
  27.9 0.0 collective-permute-done.2
  27.9 1.1 %fusion.5 = f32[12,68,132]{2,1,0:T(8,128)S(1)} fusion(bf16[2,64,132]{2,1,0:T(8,128)(2,1)} %collective-permute-done.3, bf16[2,64,132]{2,1,0:T(8,128)(2,1)} %collective-permute-done.2, bf16[8,64,2]{2,1,0:T(8,128)(2,1)S(1)} %collective-permute-done.1, bf16[8,64,128]{2,1,0:T(8,128)(2,1)S(1)} %copy-done, bf16[8,64,2]{2,1,0:T(8,128)(2,1)S(1)} %collective-permute-done), kind=kLoop, calls=%fused_computation.11 | loop fusion | flops 1938816 | bytes 633600 | tf_op jit(solution)/shard_map/convert_element_type | solution.py:35
  29.0 0.0 copy-done.1
  29.1 0.8 %add_multiply_fusion = f32[8,64,128]{2,1,0:T(8,128)S(1)} fusion(f32[12,68,132]{2,1,0:T(8,128)S(1)} %fusion.5, f32[8,64,128]{2,1,0:T(8,128)S(1)} %bitcast.29, f32[8,64,128]{2,1,0:T(8,128)S(1)} %fusion.20, f32[64,128]{1,0:T(8,128)S(1)} %copy-done.1, pred[128]{0:T(512)(128)(4,1)S(1)} %broadcast_compare_fusion), kind=kLoop, calls=%fused_computation.31 | loop fusion | flops 2490368 | bytes 3965056 | tf_op jit(solution)/shard_map/mul | solution.py:75
  29.9 0.0 copy-start.2
  29.9 0.1 multiply_reduce_fusion
  30.0 0.7 %copy-done.2 = f32[1,8,8,128]{3,2,1,0:T(8,128)S(1)} copy-done((f32[1,8,8,128]{3,2,1,0:T(8,128)S(1)}, f32[1,8,8,128]{3,2,1,0:T(8,128)}, u32[]{:S(2)}) %copy-start.2) | copy-done | bytes 32792
  30.7 11.3 %all_to_all.5 = f32[4,8,8,128]{3,2,0,1:T(8,128)S(1)} all-to-all(f32[4,8,8,128]{3,2,0,1:T(8,128)S(1)} %copy.8), channel_id=1, replica_groups=mesh['screen'=4,'depth'=8] {'depth'}, dimensions={1} | all-to-all | bytes 262144 | tf_op jit(solution)/shard_map/all_to_all | solution.py:83
  42.0 0.2 fusion.21
  42.3 0.6 %pad_maximum_fusion.4 = f32[4,8,128]{2,1,0:T(8,128)} fusion(f32[1,8,128]{2,1,0:T(8,128)S(1)} %slice_subtract_fusion.6, f32[3,8,128]{2,1,0:T(8,128)S(1)} %fusion.17), kind=kLoop, calls=%fused_computation.42 | loop fusion | flops 4096 | bytes 32768 | tf_op jit(solution)/shard_map/concatenate | solution.py:92
  (13 shorter events, 0.1 us)
Async XLA Ops:
  0.0 9.1 %copy-start.3 = (bf16[4,256]{1,0:T(4,128)(2,1)S(1)}, bf16[4,256]{1,0:T(4,128)(2,1)}, u32[]{:S(2)}) copy-start(bf16[4,256]{1,0:T(4,128)(2,1)} %param.8) | copy-start | bytes 6148
  1.1 19.7 %collective-permute-start.1 = (bf16[8,64,2]{2,1,0:T(8,128)(2,1)S(1)}, bf16[8,64,2]{2,1,0:T(8,128)(2,1)S(1)}, u32[]{:S(2)}, u32[]{:S(2)}) collective-permute-start(bf16[8,64,2]{2,1,0:T(8,128)(2,1)S(1)} %get-tuple-element.56), channel_id=1, source_target_pairs={{8,0},{16,8},{24,16},{9,1},{17,9},{25,17},{10,2},{18,10},{26,18},{... | collective-permute-start | bytes 6152 | tf_op jit(solution)/shard_map/ppermute | solution.py:20
  2.4 18.4 %collective-permute-start = (bf16[8,64,2]{2,1,0:T(8,128)(2,1)S(1)}, bf16[8,64,2]{2,1,0:T(8,128)(2,1)S(1)}, u32[]{:S(2)}, u32[]{:S(2)}) collective-permute-start(bf16[8,64,2]{2,1,0:T(8,128)(2,1)S(1)} %get-tuple-element.55), channel_id=1, source_target_pairs={{0,8},{8,16},{16,24},{1,9},{9,17},{17,25},{2,10},{10,18},{18,26},{... | collective-permute-start | bytes 6152 | tf_op jit(solution)/shard_map/ppermute | solution.py:19
  19.5 1.3 %copy-start = (bf16[8,64,128]{2,1,0:T(8,128)(2,1)S(1)}, bf16[8,64,128]{2,1,0:T(8,128)(2,1)}, u32[]{:S(2)}) copy-start(bf16[8,64,128]{2,1,0:T(8,128)(2,1)} %param.6) | copy-start | bytes 393220
  19.5 7.0 %copy-start.4 = (s32[128]{0:T(128)S(1)}, s32[128]{0:T(128)}, u32[]{:S(2)}) copy-start(s32[128]{0:T(128)} %param.9) | copy-start | bytes 1540
  21.6 6.3 %collective-permute-start.3 = (bf16[2,64,132]{2,1,0:T(8,128)(2,1)}, bf16[2,64,132]{2,1,0:T(8,128)(2,1)}, u32[]{:S(2)}, u32[]{:S(2)}) collective-permute-start(bf16[2,64,132]{2,1,0:T(8,128)(2,1)} %get-tuple-element.52), channel_id=1, source_target_pairs={{1,0},{2,1},{3,2},{4,3},{5,4},{6,5},{7,6},{9,8},{10,9},{11,10},{12... | collective-permute-start | bytes 101384 | tf_op jit(solution)/shard_map/ppermute | solution.py:20
  22.9 5.0 %collective-permute-start.2 = (bf16[2,64,132]{2,1,0:T(8,128)(2,1)}, bf16[2,64,132]{2,1,0:T(8,128)(2,1)}, u32[]{:S(2)}, u32[]{:S(2)}) collective-permute-start(bf16[2,64,132]{2,1,0:T(8,128)(2,1)} %get-tuple-element.51), channel_id=1, source_target_pairs={{0,1},{1,2},{2,3},{3,4},{4,5},{5,6},{6,7},{8,9},{9,10},{10,11},{11... | collective-permute-start | bytes 101384 | tf_op jit(solution)/shard_map/ppermute | solution.py:19
  27.9 1.2 %copy-start.1 = (f32[64,128]{1,0:T(8,128)S(1)}, f32[64,128]{1,0:T(8,128)}, u32[]{:S(2)}) copy-start(f32[64,128]{1,0:T(8,128)} %get-tuple-element.53) | copy-start | bytes 98308
  29.9 0.8 %copy-start.2 = (f32[1,8,8,128]{3,2,1,0:T(8,128)S(1)}, f32[1,8,8,128]{3,2,1,0:T(8,128)}, u32[]{:S(2)}) copy-start(f32[1,8,8,128]{3,2,1,0:T(8,128)} %get-tuple-element.54) | copy-start | bytes 98308
where the time goes:
time: 43.3 us; the launch traced here: 42.9 us
  starting transfers between devices  11.8 us (27%)
  blocking collectives  11.3 us (26%)
  matrix products  10.2 us (24%)
  other arithmetic  4.98 us (12%)
  local copies, waits for them, and re-layouts  4.43 us (10%)
    all_to_all x1, blocking collectives, on_device(): lax.all_to_all(tiles, 'depth', split_axis=1, concat_axis=1, tiled=True)  11.3 us
    dot_general x2, matrix products, lookup_block(): return jnp.dot(transfer, onehot, preferred_element_type=jnp.float32)  10.2 us
    ppermute x2, starting transfers between devices, padded_2(): before = lax.ppermute(last, axis, up)  9.22 us
    ppermute x2, starting transfers between devices, padded_2(): after = lax.ppermute(initial, axis, down)  2.57 us
    slice x2, local copies, waits for them, and re-layouts, on_device(): colour = jnp.sum(looked[:3] * weight[None], axis=1)  1.28 us
    convert_element_type x1, other arithmetic, shading_of(): field = padded.astype(jnp.float32)  1.15 us
    reshape x1, local copies, waits for them, and re-layouts, lookup(): flattened = bin_index.reshape(voxel_count // block_len, block_len)  1.11 us
    slice x1, local copies, waits for them, and re-layouts, padded_2(): last = lax.slice_in_dim(x, length - width, length, axis=dim)  1.08 us
  transfers between devices with their start and end apart: 4, of which 0 were waited for; matrix products, arithmetic and copies ran while one was open for 33% of the time, Pallas kernels for 0%

commit v1 on v0

v1 whole, which is shorter than its diff:
```python
import functools

import jax
import jax.numpy as jnp
from jax import lax
from jax.experimental import pallas as pl
from jax.experimental.pallas import tpu as pltpu
from jax.sharding import PartitionSpec as P

LIGHT_DIRECTION = (0.36, 0.48, 0.8)
AMBIENT = 0.3
DIFFUSE = 0.7
OPTICAL = 4.0
UNIT = 4096
MESH = pl.DeviceIdType.MESH
F32 = jnp.float32
BF16 = jnp.bfloat16


def lane_gather(table, lanes):
    return lax.gather(
        table,
        lanes[..., None],
        lax.GatherDimensionNumbers(
            offset_dims=(),
            collapsed_slice_dims=(1,),
            start_index_map=(1,),
            operand_batching_dims=(0,),
            start_indices_batching_dims=(0,),
        ),
        slice_sizes=(1, 1),
        mode=lax.GatherScatterMode.PROMISE_IN_BOUNDS,
    )


def stencil(distance):
    one = jnp.where(distance == 1, 8.0, jnp.where(distance == -1, -8.0, 0.0))
    two = jnp.where(distance == 2, -1.0, jnp.where(distance == -2, 1.0, 0.0))
    return (one + two).astype(BF16)


def iota(shape, axis):
    return lax.broadcasted_iota(jnp.int32, shape, axis)


def matmul(a, b, dims=((1,), (0,))):
    return lax.dot_general(a, b, (dims, ((), ())), preferred_element_type=F32)


def render_kernel(
    count, screens,
    density_hbm, bins_hbm, table_ref, side_ref, image_ref,
    dens, bins, layer_halo, edge, edge_halo, field, grad_r, grad_c, shade_in,
    send, land,
    in_sem, halo_send, halo_recv, part_send, part_recv,
):
    layers, rows, cols = density_hbm.shape
    block = rows // count
    me = lax.axis_index("depth")
    col = lax.axis_index("screen")
    has_prev, has_next = me > 0, me < count - 1
    has_left, has_right = col > 0, col < screens - 1
    powers = count & (count - 1) == 0

    def partner(k):
        return me ^ k if powers else lax.rem(me + k, count)

    load_dens = pltpu.make_async_copy(density_hbm, dens, in_sem.at[0])
    load_bins = pltpu.make_async_copy(bins_hbm, bins, in_sem.at[1])
    load_dens.start()
    load_bins.start()

    barrier = pltpu.get_barrier_semaphore()
    for k in range(1, count):
        pl.semaphore_signal(barrier, inc=1, device_id={"depth": partner(k)}, device_id_type=MESH)

    @pl.when(has_left)
    def _():
        pl.semaphore_signal(barrier, inc=1, device_id={"screen": col - 1}, device_id_type=MESH)

    @pl.when(has_right)
    def _():
        pl.semaphore_signal(barrier, inc=1, device_id={"screen": col + 1}, device_id_type=MESH)

    zeros_layer = jnp.zeros((2, rows, cols), BF16)
    zeros_edge = jnp.zeros((16, layers * rows), BF16)

    @pl.when(jnp.logical_not(has_prev))
    def _():
        layer_halo[0] = zeros_layer

    @pl.when(jnp.logical_not(has_next))
    def _():
        layer_halo[1] = zeros_layer

    @pl.when(jnp.logical_not(has_left))
    def _():
        edge_halo[pl.ds(0, 16)] = zeros_edge

    @pl.when(jnp.logical_not(has_right))
    def _():
        edge_halo[pl.ds(16, 16)] = zeros_edge

    greeted = count - 1 + has_left.astype(jnp.int32) + has_right.astype(jnp.int32)
    pl.semaphore_wait(barrier, greeted)

    def remote(src, dst, send_sem, recv_sem, target):
        return pltpu.make_async_remote_copy(
            src_ref=src, dst_ref=dst, send_sem=send_sem, recv_sem=recv_sem,
            device_id=target, device_id_type=MESH,
        )

    halos = (
        (has_next, has_prev, remote(
            density_hbm.at[pl.ds(layers - 2, 2)], layer_halo.at[0],
            halo_send.at[0], halo_recv.at[0], {"depth": me + 1})),
        (has_prev, has_next, remote(
            density_hbm.at[pl.ds(0, 2)], layer_halo.at[1],
            halo_send.at[1], halo_recv.at[1], {"depth": me - 1})),
        (has_right, has_left, remote(
            edge, edge_halo.at[pl.ds(0, 16)],
            halo_send.at[2], halo_recv.at[2], {"screen": col + 1})),
        (has_left, has_right, remote(
            edge, edge_halo.at[pl.ds(16, 16)],
            halo_send.at[3], halo_recv.at[3], {"screen": col - 1})),
    )
    for sends, _, copy in halos[:2]:
        pl.when(sends)(copy.start)

    load_dens.wait()
    flat = dens[...].reshape(layers * rows, cols)
    slot = iota((16, cols), 0)
    wanted = jnp.where(slot < 2, slot, jnp.where(slot < 4, cols - 4 + slot, -1))
    pick = (iota((16, cols), 1) == wanted).astype(F32).astype(BF16)
    edge[...] = matmul(pick, flat, ((1,), (1,))).astype(BF16)
    for sends, _, copy in halos[2:]:
        pl.when(sends)(copy.start)

    band_c = stencil(iota((cols, cols), 0) - iota((cols, cols), 1))
    band_r = stencil(iota((rows, rows), 1) - iota((rows, rows), 0))
    grad_c[...] = matmul(flat, band_c).reshape(layers, rows, cols)
    for z in range(layers):
        grad_r[z] = matmul(band_r, dens[z])
    field[pl.ds(2, layers)] = dens[...].astype(F32)

    load_bins.wait()
    units = (table_ref[...].astype(F32) * UNIT).astype(jnp.int32)
    pairs = (units[0:1] | (units[1:2] << 16), units[2:3] | (units[3:4] << 16))
    half = units.shape[1] // 2
    lows = [jnp.broadcast_to(p[:, :half], (block, half)) for p in pairs]
    highs = [jnp.broadcast_to(p[:, half:], (block, half)) for p in pairs]
    near = jnp.broadcast_to(side_ref[...] == 0, (block, cols))
    optical_scale = -OPTICAL / (layers * count) / UNIT

    def lookup_block(b, carry):
        r0 = pl.multiple_of(b * block, block)
        clear, reds, greens, blues = [], [], [], []
        for z in range(layers):
            index = bins[z, pl.ds(r0, block), :]
            lane = index & (half - 1)
            low = index < half
            pair0 = jnp.where(low, lane_gather(lows[0], lane), lane_gather(highs[0], lane))
            pair1 = jnp.where(low, lane_gather(lows[1], lane), lane_gather(highs[1], lane))
            reds.append((pair0 & 0xFFFF).astype(F32))
            greens.append((pair0 >> 16).astype(F32))
            blues.append((pair1 & 0xFFFF).astype(F32))
            clear.append(jnp.exp((pair1 >> 16).astype(F32) * optical_scale))
        ahead = [jnp.ones_like(clear[0])]
        for z in range(layers):
            ahead.append(ahead[-1] * clear[z])
        behind = jnp.ones_like(clear[0])
        for z in reversed(range(layers)):
            weight = jnp.where(near, ahead[z], behind) * ((1.0 - clear[z]) * (1.0 / UNIT))
            behind = behind * clear[z]
            shade_in[0, z, pl.ds(r0, block), :] = reds[z] * weight
            shade_in[1, z, pl.ds(r0, block), :] = greens[z] * weight
            shade_in[2, z, pl.ds(r0, block), :] = blues[z] * weight
        send[b, 3] = ahead[layers]
        return carry

    lax.fori_loop(0, count, lookup_block, 0, unroll=2 if count % 2 == 0 else 1)

    for _, arrives, copy in halos:
        pl.when(arrives)(copy.wait_recv)
    field[pl.ds(0, 2)] = layer_halo[0].astype(F32)
    field[pl.ds(layers + 2, 2)] = layer_halo[1].astype(F32)
    place = iota((32, cols), 0)
    outside = jnp.where(place == 2, -2, jnp.where(place == 3, -1, jnp.where(
        place == 16, cols, jnp.where(place == 17, cols + 1, -8))))
    band_e = stencil(outside - iota((32, cols), 1))
    grad_c[...] += matmul(edge_halo[...], band_e, ((0,), (0,))).reshape(layers, rows, cols)

    def shade_block(p):
        r0 = pl.multiple_of(p * block, block)
        f = [field[z, pl.ds(r0, block), :] for z in range(layers + 4)]
        colours = [jnp.zeros((block, cols), F32)] * 3
        for z in range(layers):
            gc = grad_c[z, pl.ds(r0, block), :]
            gr = grad_r[z, pl.ds(r0, block), :]
            gd = 8.0 * (f[z + 3] - f[z + 1]) - (f[z + 4] - f[z])
            dot = LIGHT_DIRECTION[0] * gc + LIGHT_DIRECTION[1] * gr + LIGHT_DIRECTION[2] * gd
            squared = gc * gc + gr * gr + gd * gd
            shading = AMBIENT + DIFFUSE * jnp.abs(dot) * lax.rsqrt(squared + 144.0)
            colours = [
                c + shade_in[i, z, pl.ds(r0, block), :] * shading for i, c in enumerate(colours)
            ]
        return colours

    def part_copy(k):
        p = partner(k)
        return remote(
            send.at[p], land.at[me], part_send.at[k], part_recv.at[k], {"depth": p})

    def send_block(k):
        p = partner(k)
        for c, colour in enumerate(shade_block(p)):
            send[p, c] = colour
        part_copy(k).start()

    if count <= 8:
        for k in reversed(range(1, count)):
            send_block(k)
    else:
        def step(i, carry):
            send_block(count - 1 - i)
            return carry

        lax.fori_loop(0, count - 1, step, 0)

    for c, colour in enumerate(shade_block(me)):
        land[me, c] = colour
    land[me, 3] = send[me, 3]

    for k in reversed(range(1, count)):
        part_copy(k).wait_recv()

    from_low = [jnp.zeros((block, cols), F32)] * 3
    from_high = from_low
    through = jnp.ones((block, cols), F32)
    for j in range(count):
        part_t = land[j, 3]
        through = through * part_t
        from_high = [land[j, c] + part_t * x for c, x in enumerate(from_high)]
    for j in reversed(range(count)):
        part_t = land[j, 3]
        from_low = [land[j, c] + part_t * x for c, x in enumerate(from_low)]
    for c in range(3):
        image_ref[c] = jnp.where(near, from_low[c], from_high[c])
    image_ref[3] = 1.0 - through

    for sends, _, copy in halos:
        pl.when(sends)(copy.wait_send)
    for k in range(1, count):
        part_copy(k).wait_send()


def on_device(density, bin_index, transfer, view_side):
    count, screens = lax.axis_size("depth"), lax.axis_size("screen")
    layers, rows, cols = density.shape
    block = rows // count
    vmem = pl.BlockSpec(memory_space=pltpu.VMEM)
    hbm = pl.BlockSpec(memory_space=pl.ANY)
    whole = (layers, rows, cols)
    return pl.pallas_call(
        functools.partial(render_kernel, count, screens),
        out_shape=jax.ShapeDtypeStruct((4, block, cols), F32),
        in_specs=[hbm, hbm, vmem, vmem],
        out_specs=vmem,
        scratch_shapes=[
            pltpu.VMEM(whole, BF16),
            pltpu.VMEM(whole, jnp.int32),
            pltpu.VMEM((2, 2, rows, cols), BF16),
            pltpu.VMEM((16, layers * rows), BF16),
            pltpu.VMEM((32, layers * rows), BF16),
            pltpu.VMEM((layers + 4, rows, cols), F32),
            pltpu.VMEM(whole, F32),
            pltpu.VMEM(whole, F32),
            pltpu.VMEM((3,) + whole, F32),
            pltpu.VMEM((count, 4, block, cols), F32),
            pltpu.VMEM((count, 4, block, cols), F32),
            pltpu.SemaphoreType.DMA((2,)),
            pltpu.SemaphoreType.DMA((4,)),
            pltpu.SemaphoreType.DMA((4,)),
            pltpu.SemaphoreType.DMA((count,)),
            pltpu.SemaphoreType.DMA((count,)),
        ],
        compiler_params=pltpu.CompilerParams(
            collective_id=0, has_side_effects=True, vmem_limit_bytes=40 * 2**20
        ),
        name="render",
    )(density, bin_index, transfer, view_side.reshape(1, cols))


def solution(mesh):
    placed = (P("depth", None, "screen"), P("depth", None, "screen"), P(), P("screen"))
    return jax.shard_map(
        on_device, mesh=mesh, in_specs=placed, out_specs=P(None, "depth", "screen"), check_vma=False
    )
```

time: 43.3 us -> 15.5 us (0.36)
  starting transfers between devices: 11.8 us -> 0 us
  Pallas kernels: 0 us -> 11.5 us
  blocking collectives: 11.3 us -> 0 us
  matrix products: 10.2 us -> 0 us
  other arithmetic: 4.98 us -> 0 us
  local copies, waits for them, and re-layouts: 4.43 us -> 3.8 us
    ppermute x4 -> x0, starting transfers between devices: 11.8 us -> none  [the longest x2 9.22 us: padded_2(): before = lax.ppermute(last, axis, up)]
    pallas_call x0 -> x1, Pallas kernels: none -> 11.5 us  [on_device(): pl.pallas_call(functools.partial(render_kernel, count, screens), out_shap...]
    all_to_all x1 -> x0, blocking collectives: 11.3 us -> none  [on_device(): lax.all_to_all(tiles, 'depth', split_axis=1, concat_axis=1, tiled=True)]
    dot_general x2 -> x0, matrix products: 10.2 us -> none  [lookup_block(): return jnp.dot(transfer, onehot, preferred_element_type=jnp.float32)]
    unnamed x10 -> x9, local copies, waits for them, and re-layouts: 0.69 us -> 3.8 us
    slice x6 -> x0, local copies, waits for them, and re-layouts: 2.38 us -> none  [the longest x2 1.28 us: on_device(): colour = jnp.sum(looked[:3] * weight[None], axis=1)]
    mul x2 -> x0, other arithmetic: 1.17 us -> none  [the longest x1 0.83 us: on_device(): weight = jnp.exp(-before) * opacity * shading]
    convert_element_type x1 -> x0, other arithmetic: 1.15 us -> none  [shading_of(): field = padded.astype(jnp.float32)]
  transfers between devices with their start and end apart: 4 -> 0, of which waited for: 0 -> 0; matrix products, arithmetic and copies ran while one was open for 33% -> 0% of each run, Pallas kernels for 0% -> 0%
where the time goes in v1:
time: 15.5 us; the launch traced here: 15.3 us
  Pallas kernels  11.5 us (74%)
  local copies, waits for them, and re-layouts  3.8 us (25%)
    pallas_call x1, Pallas kernels, on_device(): pl.pallas_call(functools.partial(render_kernel, count, screens), out_shap...  11.5 us
    unnamed x9, local copies, waits for them, and re-layouts  3.8 us

profile of v1, /device:TPU:0, one launch (start us, length us, event | category | flops | bytes accessed | tf_op | source)
XLA Modules:
  0.0 15.3 jit_solution(2880172234520946403)
XLA Ops:
  0.0 0.0 copy-start.3
  0.0 0.7 %copy-done.3 = s32[128]{0:T(128)S(1)} copy-done((s32[128]{0:T(128)S(1)}, s32[128]{0:T(128)}, u32[]{:S(2)}) %copy-start.3) | copy-done | bytes 536
  0.7 0.0 copy-start
  0.7 0.9 %copy-done = s32[8,64,128]{2,1,0:T(8,128)S(1)} copy-done((s32[8,64,128]{2,1,0:T(8,128)S(1)}, s32[8,64,128]{2,1,0:T(8,128)}, u32[]{:S(2)}) %copy-start) | copy-done | bytes 262168
  1.6 0.0 copy-start.1
  1.6 0.9 %copy-done.1 = bf16[8,64,128]{2,1,0:T(8,128)(2,1)S(1)} copy-done((bf16[8,64,128]{2,1,0:T(8,128)(2,1)S(1)}, bf16[8,64,128]{2,1,0:T(8,128)(2,1)}, u32[]{:S(2)}) %copy-start.1) | copy-done | bytes 131096
  2.5 0.0 copy-start.2
  2.5 0.7 %copy-done.2 = bf16[4,256]{1,0:T(4,128)(2,1)S(1)} copy-done((bf16[4,256]{1,0:T(4,128)(2,1)S(1)}, bf16[4,256]{1,0:T(4,128)(2,1)}, u32[]{:S(2)}) %copy-start.2) | copy-done | bytes 2072
  3.2 11.5 %render.1 = f32[4,8,128]{2,1,0:T(8,128)S(1)} custom-call(bf16[8,64,128]{2,1,0:T(8,128)(2,1)S(1)} %copy-done.1, s32[8,64,128]{2,1,0:T(8,128)S(1)} %copy-done, bf16[4,256]{1,0:T(4,128)(2,1)S(1)} %copy-done.2, s32[1,128]{1,0:T(1,128)S(1)} %bitcast.1), custom_call_target="tpu_custom_call" | custom-call | tf_op jit(solution)/shard_map/render/pallas_call | solution.py:264
  14.7 0.6 %copy.6 = f32[4,8,128]{2,1,0:T(8,128)} copy(f32[4,8,128]{2,1,0:T(8,128)S(1)} %render.1) | data formatting | bytes 32768
Async XLA Ops:
  0.0 0.7 %copy-start.3 = (s32[128]{0:T(128)S(1)}, s32[128]{0:T(128)}, u32[]{:S(2)}) copy-start(s32[128]{0:T(128)} %param.7) | copy-start | bytes 1540
  0.7 0.9 %copy-start = (s32[8,64,128]{2,1,0:T(8,128)S(1)}, s32[8,64,128]{2,1,0:T(8,128)}, u32[]{:S(2)}) copy-start(s32[8,64,128]{2,1,0:T(8,128)} %bins_hbm.1) | copy-start | bytes 786436
  1.6 0.9 %copy-start.1 = (bf16[8,64,128]{2,1,0:T(8,128)(2,1)S(1)}, bf16[8,64,128]{2,1,0:T(8,128)(2,1)}, u32[]{:S(2)}) copy-start(bf16[8,64,128]{2,1,0:T(8,128)(2,1)} %density_hbm.1) | copy-start | bytes 393220
  2.5 0.7 %copy-start.2 = (bf16[4,256]{1,0:T(4,128)(2,1)S(1)}, bf16[4,256]{1,0:T(4,128)(2,1)}, u32[]{:S(2)}) copy-start(bf16[4,256]{1,0:T(4,128)(2,1)} %table_ref.1) | copy-start | bytes 6148

commit v2 on v1

--- a/solution.py
+++ b/solution.py
@@ -49,8 +49,8 @@
 
 def render_kernel(
     count, screens,
-    density_hbm, bins_hbm, table_ref, side_ref, image_ref,
-    dens, bins, layer_halo, edge, edge_halo, field, grad_r, grad_c, shade_in,
+    density_hbm, bins_hbm, table_hbm, side_hbm, image_ref,
+    dens, bins, table_ref, side_ref, layer_halo, edge, edge_halo, field, grad_r, grad_c, shade_in,
     send, land,
     in_sem, halo_send, halo_recv, part_send, part_recv,
 ):
@@ -65,11 +65,6 @@
     def partner(k):
         return me ^ k if powers else lax.rem(me + k, count)
 
-    load_dens = pltpu.make_async_copy(density_hbm, dens, in_sem.at[0])
-    load_bins = pltpu.make_async_copy(bins_hbm, bins, in_sem.at[1])
-    load_dens.start()
-    load_bins.start()
-
     barrier = pltpu.get_barrier_semaphore()
     for k in range(1, count):
         pl.semaphore_signal(barrier, inc=1, device_id={"depth": partner(k)}, device_id_type=MESH)
@@ -82,6 +77,15 @@
     def _():
         pl.semaphore_signal(barrier, inc=1, device_id={"screen": col + 1}, device_id_type=MESH)
 
+    load_dens = pltpu.make_async_copy(density_hbm, dens, in_sem.at[0])
+    load_bins = pltpu.make_async_copy(bins_hbm, bins, in_sem.at[1])
+    load_table = pltpu.make_async_copy(table_hbm, table_ref, in_sem.at[2])
+    load_side = pltpu.make_async_copy(side_hbm, side_ref, in_sem.at[3])
+    load_dens.start()
+    load_table.start()
+    load_side.start()
+    load_bins.start()
+
     zeros_layer = jnp.zeros((2, rows, cols), BF16)
     zeros_edge = jnp.zeros((16, layers * rows), BF16)
 
@@ -100,6 +104,13 @@
     @pl.when(jnp.logical_not(has_right))
     def _():
         edge_halo[pl.ds(16, 16)] = zeros_edge
+
+    load_dens.wait()
+    flat = dens[...].reshape(layers * rows, cols)
+    slot = iota((16, cols), 0)
+    wanted = jnp.where(slot < 2, slot, jnp.where(slot < 4, cols - 4 + slot, -1))
+    pick = (iota((16, cols), 1) == wanted).astype(F32).astype(BF16)
+    edge[...] = matmul(pick, flat, ((1,), (1,))).astype(BF16)
 
     greeted = count - 1 + has_left.astype(jnp.int32) + has_right.astype(jnp.int32)
     pl.semaphore_wait(barrier, greeted)
@@ -124,16 +135,7 @@
             edge, edge_halo.at[pl.ds(16, 16)],
             halo_send.at[3], halo_recv.at[3], {"screen": col - 1})),
     )
-    for sends, _, copy in halos[:2]:
-        pl.when(sends)(copy.start)
-
-    load_dens.wait()
-    flat = dens[...].reshape(layers * rows, cols)
-    slot = iota((16, cols), 0)
-    wanted = jnp.where(slot < 2, slot, jnp.where(slot < 4, cols - 4 + slot, -1))
-    pick = (iota((16, cols), 1) == wanted).astype(F32).astype(BF16)
-    edge[...] = matmul(pick, flat, ((1,), (1,))).astype(BF16)
-    for sends, _, copy in halos[2:]:
+    for sends, _, copy in halos:
         pl.when(sends)(copy.start)
 
     band_c = stencil(iota((cols, cols), 0) - iota((cols, cols), 1))
@@ -143,6 +145,8 @@
         grad_r[z] = matmul(band_r, dens[z])
     field[pl.ds(2, layers)] = dens[...].astype(F32)
 
+    load_table.wait()
+    load_side.wait()
     load_bins.wait()
     units = (table_ref[...].astype(F32) * UNIT).astype(jnp.int32)
     pairs = (units[0:1] | (units[1:2] << 16), units[2:3] | (units[3:4] << 16))
@@ -259,16 +263,18 @@
     layers, rows, cols = density.shape
     block = rows // count
     vmem = pl.BlockSpec(memory_space=pltpu.VMEM)
-    hbm = pl.BlockSpec(memory_space=pl.ANY)
+    hbm = pl.BlockSpec(memory_space=pltpu.HBM)
     whole = (layers, rows, cols)
     return pl.pallas_call(
         functools.partial(render_kernel, count, screens),
         out_shape=jax.ShapeDtypeStruct((4, block, cols), F32),
-        in_specs=[hbm, hbm, vmem, vmem],
+        in_specs=[hbm] * 4,
         out_specs=vmem,
         scratch_shapes=[
             pltpu.VMEM(whole, BF16),
             pltpu.VMEM(whole, jnp.int32),
+            pltpu.VMEM(transfer.shape, BF16),
+            pltpu.VMEM((1, cols), jnp.int32),
             pltpu.VMEM((2, 2, rows, cols), BF16),
             pltpu.VMEM((16, layers * rows), BF16),
             pltpu.VMEM((32, layers * rows), BF16),
@@ -278,14 +284,14 @@
             pltpu.VMEM((3,) + whole, F32),
             pltpu.VMEM((count, 4, block, cols), F32),
             pltpu.VMEM((count, 4, block, cols), F32),
-            pltpu.SemaphoreType.DMA((2,)),
+            pltpu.SemaphoreType.DMA((4,)),
             pltpu.SemaphoreType.DMA((4,)),
             pltpu.SemaphoreType.DMA((4,)),
             pltpu.SemaphoreType.DMA((count,)),
             pltpu.SemaphoreType.DMA((count,)),
         ],
         compiler_params=pltpu.CompilerParams(
-            collective_id=0, has_side_effects=True, vmem_limit_bytes=40 * 2**20
+            collective_id=0, has_side_effects=True, vmem_limit_bytes=64 * 2**20
         ),
         name="render",
     )(density, bin_index, transfer, view_side.reshape(1, cols))

time: 15.5 us -> 13.4 us (0.86)
  local copies, waits for them, and re-layouts: 3.8 us -> 1.32 us
  Pallas kernels: 11.5 us -> 11.8 us
    unnamed x9 -> x1, local copies, waits for them, and re-layouts: 3.8 us -> 1.32 us
    pallas_call x1, Pallas kernels: 11.5 us -> 11.8 us  [on_device(): pl.pallas_call(functools.partial(render_kernel, count, screens), out_shap...]
where the time goes in v2:
time: 13.4 us; the launch traced here: 13.1 us
  Pallas kernels  11.8 us (88%)
  local copies, waits for them, and re-layouts  1.32 us (10%)
    pallas_call x1, Pallas kernels, on_device(): pl.pallas_call(functools.partial(render_kernel, count, screens), out_shap...  11.8 us
    unnamed x1, local copies, waits for them, and re-layouts  1.32 us

profile of v2, /device:TPU:0, one launch (start us, length us, event | category | flops | bytes accessed | tf_op | source)
XLA Modules:
  0.0 13.1 jit_solution(16429744044806364631)
XLA Ops:
  0.0 11.8 %render.1 = f32[4,8,128]{2,1,0:T(8,128)} custom-call(bf16[8,64,128]{2,1,0:T(8,128)(2,1)} %density_hbm.1, s32[8,64,128]{2,1,0:T(8,128)} %bins_hbm.1, bf16[4,256]{1,0:T(4,128)(2,1)} %table_hbm.1, s32[1,128]{1,0:T(1,128)} %bitcast.1), custom_call_target="tpu_custom_call" | custom-call | tf_op jit(solution)/shard_map/render/pallas_call | solution.py:268
  11.8 1.3 %copy.6 = f32[4,8,128]{2,1,0:T(8,128)} copy(f32[4,8,128]{2,1,0:T(8,128)} %render.1) | data formatting | bytes 32768

commit v3 on v2

--- a/solution.py
+++ b/solution.py
@@ -12,6 +12,7 @@
 DIFFUSE = 0.7
 OPTICAL = 4.0
 UNIT = 4096
+LEVELS = 65534
 MESH = pl.DeviceIdType.MESH
 F32 = jnp.float32
 BF16 = jnp.bfloat16
@@ -51,7 +52,7 @@
     count, screens,
     density_hbm, bins_hbm, table_hbm, side_hbm, image_ref,
     dens, bins, table_ref, side_ref, layer_halo, edge, edge_halo, field, grad_r, grad_c, shade_in,
-    send, land,
+    extinct, send, land,
     in_sem, halo_send, halo_recv, part_send, part_recv,
 ):
     layers, rows, cols = density_hbm.shape
@@ -159,6 +160,7 @@
     def lookup_block(b, carry):
         r0 = pl.multiple_of(b * block, block)
         clear, reds, greens, blues = [], [], [], []
+        total = jnp.zeros((block, cols), F32)
         for z in range(layers):
             index = bins[z, pl.ds(r0, block), :]
             lane = index & (half - 1)
@@ -168,9 +170,11 @@
             reds.append((pair0 & 0xFFFF).astype(F32))
             greens.append((pair0 >> 16).astype(F32))
             blues.append((pair1 & 0xFFFF).astype(F32))
-            clear.append(jnp.exp((pair1 >> 16).astype(F32) * optical_scale))
+            extinction = (pair1 >> 16).astype(F32)
+            total = total + extinction
+            clear.append(jnp.exp(extinction * optical_scale))
         ahead = [jnp.ones_like(clear[0])]
-        for z in range(layers):
+        for z in range(layers - 1):
             ahead.append(ahead[-1] * clear[z])
         behind = jnp.ones_like(clear[0])
         for z in reversed(range(layers)):
@@ -179,7 +183,7 @@
             shade_in[0, z, pl.ds(r0, block), :] = reds[z] * weight
             shade_in[1, z, pl.ds(r0, block), :] = greens[z] * weight
             shade_in[2, z, pl.ds(r0, block), :] = blues[z] * weight
-        send[b, 3] = ahead[layers]
+        extinct[pl.ds(r0, block), :] = total
         return carry
 
     lax.fori_loop(0, count, lookup_block, 0, unroll=2 if count % 2 == 0 else 1)
@@ -208,7 +212,11 @@
             colours = [
                 c + shade_in[i, z, pl.ds(r0, block), :] * shading for i, c in enumerate(colours)
             ]
-        return colours
+        total = extinct[pl.ds(r0, block), :]
+        spread = LEVELS / (1.0 - jnp.exp(total * optical_scale))
+        codes = [jnp.minimum(c * spread, LEVELS) - (LEVELS // 2 - 0.5) for c in colours]
+        codes = jnp.concatenate(codes + [total - layers * UNIT // 2], axis=0)
+        return jnp.floor(codes).astype(jnp.int32).astype(jnp.int16)
 
     def part_copy(k):
         p = partner(k)
@@ -217,8 +225,7 @@
 
     def send_block(k):
         p = partner(k)
-        for c, colour in enumerate(shade_block(p)):
-            send[p, c] = colour
+        send[p] = shade_block(p)
         part_copy(k).start()
 
     if count <= 8:
@@ -231,23 +238,28 @@
 
         lax.fori_loop(0, count - 1, step, 0)
 
-    for c, colour in enumerate(shade_block(me)):
-        land[me, c] = colour
-    land[me, 3] = send[me, 3]
+    land[me] = shade_block(me)
 
     for k in reversed(range(1, count)):
         part_copy(k).wait_recv()
 
+    parts = []
+    for j in range(count):
+        codes = land[j].astype(jnp.int32).astype(F32)
+        total = codes[3 * block:] + layers * UNIT // 2
+        part_t = jnp.exp(total * optical_scale)
+        spread = (1.0 - part_t) * (1.0 / LEVELS)
+        parts.append([
+            (codes[c * block:(c + 1) * block] + LEVELS // 2) * spread for c in range(3)
+        ] + [part_t])
     from_low = [jnp.zeros((block, cols), F32)] * 3
     from_high = from_low
     through = jnp.ones((block, cols), F32)
-    for j in range(count):
-        part_t = land[j, 3]
-        through = through * part_t
-        from_high = [land[j, c] + part_t * x for c, x in enumerate(from_high)]
-    for j in reversed(range(count)):
-        part_t = land[j, 3]
-        from_low = [land[j, c] + part_t * x for c, x in enumerate(from_low)]
+    for part in parts:
+        through = through * part[3]
+        from_high = [part[c] + part[3] * x for c, x in enumerate(from_high)]
+    for part in reversed(parts):
+        from_low = [part[c] + part[3] * x for c, x in enumerate(from_low)]
     for c in range(3):
         image_ref[c] = jnp.where(near, from_low[c], from_high[c])
     image_ref[3] = 1.0 - through
@@ -282,8 +294,9 @@
             pltpu.VMEM(whole, F32),
             pltpu.VMEM(whole, F32),
             pltpu.VMEM((3,) + whole, F32),
-            pltpu.VMEM((count, 4, block, cols), F32),
-            pltpu.VMEM((count, 4, block, cols), F32),
+            pltpu.VMEM((rows, cols), F32),
+            pltpu.VMEM((count, 4 * block, cols), jnp.int16),
+            pltpu.VMEM((count, 4 * block, cols), jnp.int16),
             pltpu.SemaphoreType.DMA((4,)),
             pltpu.SemaphoreType.DMA((4,)),
             pltpu.SemaphoreType.DMA((4,)),

time: 13.4 us -> 13.2 us (0.985)
    pallas_call x1, Pallas kernels: 11.8 us -> 11.7 us  [on_device(): pl.pallas_call(functools.partial(render_kernel, count, screens), out_shap...]
where the time goes in v3:
time: 13.2 us; the launch traced here: 13 us
  Pallas kernels  11.7 us (89%)
  local copies, waits for them, and re-layouts  1.32 us (10%)
    pallas_call x1, Pallas kernels, on_device(): pl.pallas_call(functools.partial(render_kernel, count, screens), out_shap...  11.7 us
    unnamed x1, local copies, waits for them, and re-layouts  1.32 us

profile of v3, /device:TPU:0, one launch (start us, length us, event | category | flops | bytes accessed | tf_op | source)
XLA Modules:
  0.0 13.0 jit_solution(18260376578517846304)
XLA Ops:
  0.0 11.7 %render.1 = f32[4,8,128]{2,1,0:T(8,128)} custom-call(bf16[8,64,128]{2,1,0:T(8,128)(2,1)} %density_hbm.1, s32[8,64,128]{2,1,0:T(8,128)} %bins_hbm.1, bf16[4,256]{1,0:T(4,128)(2,1)} %table_hbm.1, s32[1,128]{1,0:T(1,128)} %bitcast.1), custom_call_target="tpu_custom_call" | custom-call | tf_op jit(solution)/shard_map/render/pallas_call | solution.py:280
  11.7 1.3 %copy.6 = f32[4,8,128]{2,1,0:T(8,128)} copy(f32[4,8,128]{2,1,0:T(8,128)} %render.1) | data formatting | bytes 32768
